TPU v7x, 256 devices: a whole 4x4x8 slice. The times are simulated.
256 devices in a mesh: cfg: 8 (over z_hi, core), row: 8 (over y, z_lo), col: 4 (over x).
Axes of the slice: x: 4, y: 4, z: 8 (z_hi: 4, z_lo: 2; z = z_hi * 2 + z_lo), core: 2. Of those that a mesh axis runs over, the one named last changes fastest.
Arguments:
- sigma_above: float32 [8, 4, 4, 8, 16, 4, 512], P('cfg', None, None, 'row', None, None, 'col'), as said below
- panels: float32 [8, 4, 8, 4, 8, 16, 512], P('cfg', None, None, None, 'row', None, 'col'), may hold values from -0.046875 to 0.046875
- diag_inverse: float32 [8, 4, 4, 8, 16, 512], P('cfg', None, None, 'row', None, 'col'), as said below
- pattern: int32 [8, 4], replicated, may hold values from 0 to 1, as said below
- cfg_weight: float32 [8], P('cfg'), may hold values from 0.2 to 1
Outputs:
- selected: float32 [8, 4, 8, 16, 4, 512], P('cfg', None, 'row', None, None, 'col')
Inputs may be any that keep to these rules, and one draw needn't show every extreme that they name: pattern[l, j] is 0 for l <= j and 1 for l = j + 1; for l > j + 1 it is 0 or 1. Each configuration's sigma_above is a symmetric matrix of order 4 * 512. Each diag_inverse[g, j] is a symmetric matrix of order 512.
All inputs are finite; a program needn't handle non-finite values.
Results may differ from a plain program's by a relative error of at most 0.0001.
Values sent between devices are 32-bit elements; how exact they have to be, the bound alone decides.
A program may use at most 64 MiB of HBM per device.

v0:
```python
import jax
import jax.numpy as jnp
from jax import lax
from jax.sharding import PartitionSpec as P


def arrange_pieces(tiles, grid_rows, grid_cols, sub_rows):
    blocks = tiles.shape[0]
    shaped = tiles.reshape(blocks, grid_cols, sub_rows, grid_rows, sub_rows)
    return shaped.transpose(3, 1, 0, 2, 4).reshape(
        grid_rows * grid_cols, blocks, sub_rows, sub_rows
    )


def settle_pieces(received, grid_rows, grid_cols, sub_rows):
    blocks = received.shape[1]
    shaped = received.reshape(grid_rows, grid_cols, blocks, sub_rows, sub_rows)
    return shaped.transpose(2, 1, 4, 0, 3).reshape(
        blocks, grid_cols * sub_rows, grid_rows * sub_rows
    )


def local(sigma_above, panels, diag_inverse, pattern, cfg_weight):
    grid_rows = lax.axis_size("row")
    groups = lax.axis_size("cfg")
    grid_cols = sigma_above.shape[2]
    sub_rows = sigma_above.shape[4]
    tile_cols = sigma_above.shape[6]
    tile_rows = grid_cols * sub_rows
    above_blocks = sigma_above.shape[1]
    blocks = pattern.shape[0]
    window = pattern.shape[1]
    local_blocks = blocks // groups
    full_width = tile_cols * grid_cols
    highest = lax.Precision.HIGHEST
    pattern_f = pattern.astype(jnp.float32)
    selector = pattern_f + jnp.eye(blocks, window, dtype=jnp.float32)
    sigma_state = jnp.zeros((blocks, tile_rows, blocks, tile_cols), jnp.float32)
    known = sigma_above[0].reshape(above_blocks, tile_rows, above_blocks, tile_cols)
    sigma_state = sigma_state.at[window:, :, window:, :].set(known)
    for column in reversed(range(window)):
        first = column + 1
        later = blocks - first
        panel_tile = (
            panels[0, column, first:].reshape(later, tile_rows, tile_cols)
            * pattern_f[first:, column][:, None, None]
        )
        flat_state = sigma_state[first:, :, first:, :].reshape(later * tile_rows, later * tile_cols)
        gathered = lax.all_gather(panel_tile, "col", axis=2, tiled=True)
        flat_panel = gathered.reshape(later * tile_rows, full_width)
        products = lax.dot_general(
            flat_panel,
            flat_state,
            (((0,), (0,)), ((), ())),
            precision=highest,
            preferred_element_type=jnp.float32,
        )
        products = products.reshape(grid_cols, grid_rows, sub_rows, later, tile_cols)
        summed = lax.psum_scatter(products, "row", scatter_dimension=1, tiled=True)
        row_later = -summed.reshape(tile_rows, later, tile_cols)
        pieces = arrange_pieces(row_later.transpose(1, 0, 2), grid_rows, grid_cols, sub_rows)
        received = lax.all_to_all(pieces, ("row", "col"), split_axis=0, concat_axis=0, tiled=True)
        col_later = settle_pieces(received, grid_rows, grid_cols, sub_rows)
        inner_terms = lax.dot_general(
            flat_panel,
            col_later.reshape(later * tile_rows, tile_cols),
            (((0,), (0,)), ((), ())),
            precision=highest,
            preferred_element_type=jnp.float32,
        )
        inner_terms = inner_terms.reshape(grid_cols, grid_rows, sub_rows, tile_cols)
        correction = lax.psum_scatter(inner_terms, "row", scatter_dimension=1, tiled=True).reshape(
            tile_rows, tile_cols
        )
        diagonal = diag_inverse[0, column].reshape(tile_rows, tile_cols) - correction
        sigma_state = sigma_state.at[column, :, first:, :].set(row_later)
        sigma_state = sigma_state.at[first:, :, column, :].set(col_later)
        sigma_state = sigma_state.at[column, :, column, :].set(diagonal)
    share_all = sigma_state[:, :, :window, :] * (selector * cfg_weight[0])[:, None, :, None]
    weighted_sum = lax.psum_scatter(share_all, "cfg", scatter_dimension=0, tiled=True)
    return weighted_sum.reshape(local_blocks, grid_cols, 1, sub_rows, window, tile_cols)


def solution(mesh):
    return jax.shard_map(
        local,
        mesh=mesh,
        in_specs=(
            P("cfg", None, None, "row", None, None, "col"),
            P("cfg", None, None, None, "row", None, "col"),
            P("cfg", None, None, "row", None, "col"),
            P(),
            P("cfg"),
        ),
        out_specs=P("cfg", None, "row", None, None, "col"),
        check_vma=False,
    )
```

profile of v0, /device:TPU:6, one launch (start us, length us, event | category | flops | bytes accessed | tf_op | source)
XLA Modules:
  0.0 937.2 jit_solution(8201129600709938030)
XLA Ops:
  8.4 13.4 %all_gather.12 = f32[4,64,512]{2,1,0:T(8,128)S(1)} all-gather(f32[4,64,128]{2,1,0:T(8,128)S(1)} %broadcast_multiply_fusion.3), channel_id=1, replica_groups=mesh['cfg'=8,'row'=8,'col'=4] {'col'}, dimensions={2}, use_global_device_ids=true | all-gather | bytes 655360 | tf_op jit(solution)/shard_map/all_gather | solution.py:49
  26.0 86.4 %all-reduce.18.cloned.1.call-done = f32[4,8,16,4,128]{4,2,3,1,0:T(8,128)} async-done(((f32[4,8,16,4,128]{4,2,3,1,0:T(8,128)}), f32[4,8,16,4,128]{4,2,3,1,0:T(8,128)}) %all-reduce.18.cloned.1.call-update) | async-done | bytes 1048592
  115.5 6.6 all-to-all-start
  122.2 13.0 %all_gather.13 = f32[5,64,512]{2,1,0:T(8,128)S(1)} all-gather(f32[5,64,128]{2,1,0:T(8,128)S(1)} %broadcast_multiply_fusion.2), channel_id=1, replica_groups=mesh['cfg'=8,'row'=8,'col'=4] {'col'}, dimensions={2}, use_global_device_ids=true | all-gather | bytes 819200 | tf_op jit(solution)/shard_map/all_gather | solution.py:49
  144.9 78.7 %all-reduce.20.cloned.1.call-done = f32[4,8,16,128]{3,2,1,0:T(8,128)} async-done(((f32[4,8,16,128]{3,2,1,0:T(8,128)}), f32[4,8,16,128]{3,2,1,0:T(8,128)}) %all-reduce.20.cloned.1.call-update) | async-done | bytes 262160
  228.9 4.7 fusion.12
  235.4 85.8 %all-reduce.22.cloned.1.call-done = f32[4,8,16,5,128]{4,2,3,1,0:T(8,128)} async-done(((f32[4,8,16,5,128]{4,2,3,1,0:T(8,128)}), f32[4,8,16,5,128]{4,2,3,1,0:T(8,128)}) %all-reduce.22.cloned.1.call-update) | async-done | bytes 1310736
  326.9 5.9 all-to-all-start.1
  333.9 14.5 %all_gather.14 = f32[6,64,512]{2,1,0:T(8,128)S(1)} all-gather(f32[6,64,128]{2,1,0:T(8,128)S(1)} %broadcast_multiply_fusion.1), channel_id=1, replica_groups=mesh['cfg'=8,'row'=8,'col'=4] {'col'}, dimensions={2}, use_global_device_ids=true | all-gather | bytes 983040 | tf_op jit(solution)/shard_map/all_gather | solution.py:49
  360.5 76.3 %all-reduce.24.cloned.1.call-done = f32[4,8,16,128]{3,2,1,0:T(8,128)} async-done(((f32[4,8,16,128]{3,2,1,0:T(8,128)}), f32[4,8,16,128]{3,2,1,0:T(8,128)}) %all-reduce.24.cloned.1.call-update) | async-done | bytes 262160
  443.0 5.1 fusion.13
  449.2 90.0 %all-reduce.26.cloned.1.call-done = f32[4,8,16,6,128]{4,2,3,1,0:T(8,128)} async-done(((f32[4,8,16,6,128]{4,2,3,1,0:T(8,128)}), f32[4,8,16,6,128]{4,2,3,1,0:T(8,128)}) %all-reduce.26.cloned.1.call-update) | async-done | bytes 1572880
  542.3 2.9 copy.112
  547.8 6.7 all-to-all-start.2
  554.7 14.5 %all_gather.15 = f32[7,64,512]{2,1,0:T(8,128)} all-gather(f32[7,64,128]{2,1,0:T(8,128)S(1)} %broadcast_multiply_fusion), channel_id=1, replica_groups=mesh['cfg'=8,'row'=8,'col'=4] {'col'}, dimensions={2}, use_global_device_ids=true | all-gather | bytes 1146880 | tf_op jit(solution)/shard_map/all_gather | solution.py:49
  574.5 3.1 copy.113
  583.9 78.2 %all-reduce.28.cloned.1.call-done = f32[4,8,16,128]{3,2,1,0:T(8,128)} async-done(((f32[4,8,16,128]{3,2,1,0:T(8,128)}), f32[4,8,16,128]{3,2,1,0:T(8,128)}) %all-reduce.28.cloned.1.call-update) | async-done | bytes 262160
  668.7 6.3 fusion
  675.0 98.9 %all-reduce.30.cloned.1.call-done = f32[4,8,16,7,128]{4,2,3,1,0:T(8,128)} async-done(((f32[4,8,16,7,128]{4,2,3,1,0:T(8,128)}), f32[4,8,16,7,128]{4,2,3,1,0:T(8,128)}) %all-reduce.30.cloned.1.call-update) | async-done | bytes 1835024
  777.2 3.1 copy.120
  783.1 6.2 all-to-all-start.3
  792.4 3.8 all-to-all-done.3
  813.4 74.7 %all-reduce.32.cloned.1.call-done = f32[4,8,16,128]{3,2,1,0:T(8,128)} async-done(((f32[4,8,16,128]{3,2,1,0:T(8,128)}), f32[4,8,16,128]{3,2,1,0:T(8,128)}) %all-reduce.32.cloned.1.call-update) | async-done | bytes 262160
  890.6 38.2 %reduce-scatter.14.cloned.1.call-done = f32[1,64,4,128]{3,1,2,0:T(8,128)} async-done(((f32[8,64,4,128]{3,1,2,0:T(8,128)}), f32[1,64,4,128]{3,1,2,0:T(8,128)}) %reduce-scatter.14.cloned.1.call-update) | async-done | bytes 131088 | tf_op jit(solution)/shard_map/reduce_scatter | solution.py:80
  (141 shorter events, 105.6 us)
Async XLA Ops:
  6.5 15.5 %copy-start.3 = (f32[1,4,4,1,16,4,128]{6,5,4,3,2,1,0:T(4,128)S(1)}, f32[1,4,4,1,16,4,128]{6,5,4,3,2,1,0:T(4,128)}, u32[]{:S(2)}) copy-start(f32[1,4,4,1,16,4,128]{6,5,4,3,2,1,0:T(4,128)} %param.31) | copy-start | bytes 1572868
  6.5 105.9 %all-reduce.18.cloned.1.call-start = ((), (), s32[]{:S(2)}) async-start(), calls=%async_computation.6 | async-start | bytes 2097152
  22.0 2.3 copy-start.2
  22.2 3.0 copy-start.10
  115.5 21.9 %all-to-all-start = ((f32[32,1,1024]{2,1,0:T(1,128)}), f32[32,1,1024]{2,1,0:T(1,128)S(1)}, u32[]{:S(2)}, u32[]{:S(2)}) async-start(f32[32,1,1024]{2,1,0:T(1,128)} %reshape.767), calls=%async_computation | async-start | bytes 262144 | tf_op jit(solution)/shard_map/all_to_all | solution.py:62
  122.1 101.4 %all-reduce.20.cloned.1.call-start = ((), (), s32[]{:S(2)}) async-start(), calls=%async_computation.7 | async-start | bytes 524288
  135.3 1.5 copy-start.5
  144.5 176.8 %all-reduce.22.cloned.1.call-start = ((), (), s32[]{:S(2)}) async-start(), calls=%async_computation.8 | async-start | bytes 2621440
  225.5 3.5 copy-start.1
  322.7 1.5 copy-start.4
  326.9 22.6 %all-to-all-start.1 = ((f32[32,1,1280]{2,1,0:T(1,128)}), f32[32,1,1280]{2,1,0:T(1,128)S(1)}, u32[]{:S(2)}, u32[]{:S(2)}) async-start(f32[32,1,1280]{2,1,0:T(1,128)} %reshape.769), calls=%async_computation.1 | async-start | bytes 327680 | tf_op jit(solution)/shard_map/all_to_all | solution.py:62
  332.8 103.9 %all-reduce.24.cloned.1.call-start = ((), (), s32[]{:S(2)}) async-start(), calls=%async_computation.9 | async-start | bytes 524288
  357.5 181.6 %all-reduce.26.cloned.1.call-start = ((), (), s32[]{:S(2)}) async-start(), calls=%async_computation.10 | async-start | bytes 3145728
  440.2 2.8 copy-start
  547.8 22.9 %all-to-all-start.2 = ((f32[32,1,1536]{2,1,0:T(1,128)}), f32[32,1,1536]{2,1,0:T(1,128)}, u32[]{:S(2)}, u32[]{:S(2)}) async-start(f32[32,1,1536]{2,1,0:T(1,128)} %reshape.771), calls=%async_computation.2 | async-start | bytes 393216 | tf_op jit(solution)/shard_map/all_to_all | solution.py:62
  554.6 107.5 %all-reduce.28.cloned.1.call-start = ((), (), s32[]{:S(2)}) async-start(), calls=%async_computation.11 | async-start | bytes 524288
  582.0 81.5 %copy-start.7 = (f32[1,1,4,1,16,128]{5,4,3,2,1,0:T(8,128)S(1)}, f32[1,1,4,1,16,128]{5,4,3,2,1,0:T(8,128)}, u32[]{:S(2)}) copy-start(f32[1,1,4,1,16,128]{5,4,3,2,1,0:T(8,128)} %get-tuple-element.164) | copy-start | bytes 98308
  582.0 191.9 %all-reduce.30.cloned.1.call-start = ((), (), s32[]{:S(2)}) async-start(), calls=%async_computation.12 | async-start | bytes 3670016
  780.2 10.7 %copy-start.8 = (s32[8,4]{0,1:T(4,128)S(1)}, s32[8,4]{0,1:T(4,128)}, u32[]{:S(2)}) copy-start(s32[8,4]{0,1:T(4,128)} %param.34) | copy-start | bytes 388
  780.2 10.8 %copy-start.9 = (s32[4]{0:T(128)S(1)}, s32[4]{0:T(128)}, u32[]{:S(2)}) copy-start(s32[4]{0:T(128)} %constant.391.clone.1) | copy-start | bytes 52
  783.1 13.2 %all-to-all-start.3 = ((f32[32,1,1792]{2,1,0:T(1,128)}), f32[32,1,1792]{2,1,0:T(1,128)}, u32[]{:S(2)}, u32[]{:S(2)}) async-start(f32[32,1,1792]{2,1,0:T(1,128)} %reshape.773), calls=%async_computation.3 | async-start | bytes 458752 | tf_op jit(solution)/shard_map/all_to_all | solution.py:62
  789.3 98.8 %all-reduce.32.cloned.1.call-start = ((), (), s32[]{:S(2)}) async-start(), calls=%async_computation.13 | async-start | bytes 524288
  810.0 79.5 %copy-start.6 = (f32[1,1,4,1,16,128]{5,4,3,2,1,0:T(8,128)S(1)}, f32[1,1,4,1,16,128]{5,4,3,2,1,0:T(8,128)}, u32[]{:S(2)}) copy-start(f32[1,1,4,1,16,128]{5,4,3,2,1,0:T(8,128)} %get-tuple-element.161) | copy-start | bytes 98308
  810.0 118.8 %reduce-scatter.14.cloned.1.call-start = ((), (), s32[]{:S(2)}) async-start(), calls=%async_computation.5 | async-start | bytes 1179648 | tf_op jit(solution)/shard_map/reduce_scatter | solution.py:80
Sparse Core Ops, SparseCore 0:
  24.4 87.9 all-reduce.17
  144.6 78.9 all-reduce.19
  233.8 87.3 all-reduce.21
  357.7 79.0 all-reduce.23
  448.2 90.8 all-reduce.25
  582.1 79.9 all-reduce.27
  675.1 98.6 all-reduce.29
  810.1 77.9 all-reduce.31
  890.7 38.0 reduce-scatter.13
where the time goes:
time: 948 us; the launch traced here: 937 us
  waiting for transfers between devices  711 us (75%)
  local copies, waits for them, and re-layouts  83 us (9%)
  blocking collectives  55.4 us (6%)
  matrix products  28.4 us (3%)
  starting transfers between devices  26 us (3%)
  other arithmetic  18.7 us (2%)
  between operations  14.5 us (2%)
    unnamed x17, waiting for transfers between devices  669 us
    all_gather x4, blocking collectives, local(): gathered = lax.all_gather(panel_tile, 'col', axis=2, tiled=True)  55.4 us
    reduce_scatter x1, waiting for transfers between devices, local(): lax.psum_scatter(share_all, 'cfg', scatter_dimension=0, tiled=True)  38.2 us
    all_to_all x4, starting transfers between devices, local(): lax.all_to_all(pieces, ('row', 'col'), split_axis=0, concat_axis=0, tiled...  25.5 us
    unnamed x40, local copies, waits for them, and re-layouts  24.9 us
  transfers between devices with their start and end apart: 13, of which 10 were waited for; matrix products, arithmetic and copies ran while one was open for 2% of the time, Pallas kernels for 0%

commit v1 on v0

v1 whole, which is shorter than its diff:
```python
import jax
import jax.numpy as jnp
from jax import lax
from jax.experimental import pallas as pl
from jax.experimental.pallas import tpu as pltpu
from jax.sharding import PartitionSpec as P

MESH = pl.DeviceIdType.MESH
F32 = jnp.float32
BF16 = jnp.bfloat16
W = 4
NB = 8
ROWS = 8
COLS = 4
GROUPS = 4
SUB = 16
TR = 64
TC = 128
FULL = 512
WINDOW_BLOCKS = ((3, 2), (3, 1), (2, 1), (3, 0), (2, 0), (1, 0))
WINDOW_PHASES = ((0, 1), (1, 2), (3, 3))


def split(x):
    hi = x.astype(BF16)
    return hi, (x - hi.astype(F32)).astype(BF16)


def dot3(ah, al, bh, bl, dims=(((1,), (0,)), ((), ()))):
    def one(a, b):
        return lax.dot_general(a, b, dims, preferred_element_type=F32)

    return one(ah, bh) + (one(ah, bl) + one(al, bh))


def kernel(
    a_ref, u_ref, d_ref, pat_ref, w_ref, out_ref,
    tr, zx0, zx1, zx2, zx3, zr0, zr1, zr2, zr3, ax, dg,
    ah, al, dh, dl, th, tl, zh0, zh1, zh2, zh3, zl0, zl1, zl2, zl3, bh, bl, qh, ql,
    pw, pa, rw, ra, gw, hb, kb,
    send, recv, send1, recv1,
):
    zx, zr = (zx0, zx1, zx2, zx3), (zr0, zr1, zr2, zr3)
    zh, zl = (zh0, zh1, zh2, zh3), (zl0, zl1, zl2, zl3)
    g, r, c = lax.axis_index("cfg"), lax.axis_index("row"), lax.axis_index("col")
    z_hi, core = lax.div(g, 2), lax.rem(g, 2)
    other = 1 - core
    row_peers = [lax.rem(r + d, ROWS) for d in range(1, ROWS)]
    col_peers = [lax.rem(c + d, COLS) for d in range(1, COLS)]
    z_peers = [lax.rem(z_hi + d, 4) for d in range(1, 4)]
    sibling = {"cfg": 2 * z_hi + other}

    barrier = pltpu.get_barrier_semaphore()
    everyone = [{"row": p} for p in row_peers] + [{"col": p} for p in col_peers]
    everyone += [{"cfg": 2 * p + core} for p in z_peers] + [sibling]
    for peer in everyone:
        pl.semaphore_signal(barrier, inc=1, device_id=peer, device_id_type=MESH)
    pl.semaphore_wait(barrier, len(everyone))

    waits = []

    def put(src, dst, phase, peer):
        pltpu.make_async_remote_copy(
            src_ref=src, dst_ref=dst, send_sem=send.at[phase], recv_sem=recv.at[phase],
            device_id=peer, device_id_type=MESH,
        ).start()

    def take(phase, ref):
        pltpu.make_async_copy(ref, ref, recv.at[phase]).wait()
        waits.append((phase, ref))

    def over_rows(src, dst, phase):
        for p in row_peers:
            put(src, dst, phase, {"row": p})

    def over_cols(src, dst, phase):
        for p in col_peers:
            put(src, dst, phase, {"col": p})

    X, R, T, A, D, F2, F3 = 0, 4, 8, 11, 12, 13, 17

    def panel(k, j):
        return u_ref[j, k] * pat_ref[k, j].astype(F32)

    def send_z(j):
        over_cols(zx[j].at[c], zx[j].at[c], X + j)
        over_rows(zx[j].at[c], zr[j].at[r], R + j)

    def take_x(j):
        take(X + j, zx[j].at[pl.ds(0, COLS - 1)])
        for q in range(COLS):
            hi, lo = split(zx[j][q].reshape(-1, TC))
            zh[j][:, q * TC:(q + 1) * TC] = hi
            zl[j][:, q * TC:(q + 1) * TC] = lo

    def take_t(phase):
        first, count = WINDOW_PHASES[phase]
        take(T + phase, tr.at[pl.ds(0, ROWS - 1), pl.ds(first, count)])
        for s in range(first, first + count):
            for q in range(ROWS):
                hi, lo = split(tr[q, s].reshape(GROUPS, SUB, TC))
                th[s, :, q] = hi
                tl[s, :, q] = lo

    for s, (i, j) in enumerate(WINDOW_BLOCKS):
        tr[r, s] = panel(i, j)
    for k in range(W, NB):
        block = -panel(k, 3)
        zx[3][c, k - 4] = block
        zr[3][r, k - 4] = block

    def send_t(phase):
        first, count = WINDOW_PHASES[phase]
        piece = tr.at[r, pl.ds(first, count)]
        over_rows(piece, piece, T + phase)

    send_t(0)
    over_cols(zx[3].at[c], zx[3].at[c], X + 3)
    send_t(1)
    over_rows(zx[3].at[c], zr[3].at[r], R + 3)
    send_t(2)
    for k in range(1, W):
        dg[c, k - 1] = d_ref[k]
    over_cols(dg.at[c], dg.at[c], D)
    over_cols(a_ref, ax.at[c], A)
    ax[c] = a_ref[...]

    for j in (2, 1, 0):
        take_t(2 - j)
        take_x(j + 1)
        blocks = NB - 1 - j
        acc = [-panel(k, j) for k in range(j + 1, NB)]
        for i in range(j + 1, W):
            s = WINDOW_BLOCKS.index((i, j))
            part = dot3(
                zh[i][...], zl[i][...], th[s].reshape(FULL, TC), tl[s].reshape(FULL, TC)
            ).reshape(NB - 1 - i, TR, TC)
            for k in range(i + 1, NB):
                acc[k - j - 1] -= part[k - i - 1]
        for m in range(blocks):
            zx[j][c, m] = acc[m]
            zr[j][r, m] = acc[m]
        send_z(j)

    take(A, ax.at[pl.ds(0, COLS - 1)])
    for q in range(COLS):
        for m in range(4):
            hi, lo = split(ax[q, :, m, :])
            lanes = slice(m * FULL + q * TC, m * FULL + (q + 1) * TC)
            ah[:, lanes] = hi
            al[:, lanes] = lo
    take(D, dg.at[pl.ds(0, COLS - 1)])
    for q in range(COLS):
        for k in range(3):
            hi, lo = split(dg[q, k])
            dh[k, :, q * TC:(q + 1) * TC] = hi
            dl[k, :, q * TC:(q + 1) * TC] = lo

    weight = w_ref[0]

    def column(j):
        blocks = NB - 1 - j
        take(R + j, zr[j].at[pl.ds(0, ROWS - 1)])
        for q in range(ROWS):
            hi, lo = split(zr[j][q].reshape(blocks, GROUPS, SUB, TC))
            bh[0:blocks, :, q] = hi
            bl[0:blocks, :, q] = lo
        first = blocks - 4
        q_above = weight * dot3(
            ah[...], al[...],
            bh[first:blocks].reshape(4 * FULL, TC), bl[first:blocks].reshape(4 * FULL, TC),
        )
        hi, lo = split(q_above)
        qh[first * TR:blocks * TR, :] = hi
        ql[first * TR:blocks * TR, :] = lo
        q_above = q_above.reshape(4, TR, TC)
        for m in range(4):
            pa[j, m] = q_above[m]
        inside = []
        for m in range(first):
            k = j + 1 + m
            q_in = weight * dot3(
                dh[k - 1], dl[k - 1], bh[m].reshape(FULL, TC), bl[m].reshape(FULL, TC)
            )
            hi, lo = split(q_in)
            qh[m * TR:(m + 1) * TR, :] = hi
            ql[m * TR:(m + 1) * TR, :] = lo
            inside.append(q_in)
        for l in range(j, W):
            start = (l - j) * TR
            part = dot3(
                zh[l][...], zl[l][...],
                qh[start:blocks * TR, :], ql[start:blocks * TR, :],
                (((0,), (0,)), ((), ())),
            ).reshape(GROUPS, ROWS, SUB, TC)
            for q in range(ROWS):
                pw[j, l, q] = part[:, q].reshape(TR, TC)
            pw[j, l, r] += weight * d_ref[j] if l == j else inside[l - j - 1]

    pairs = []

    def to_sibling(slot, src, dst):
        copy = pltpu.make_async_remote_copy(
            src_ref=src, dst_ref=dst, send_sem=send1.at[slot], recv_sem=recv1.at[slot],
            device_id=sibling, device_id_type=MESH,
        )
        copy.start()
        pairs.append(copy)
        return copy

    def finish(lo, count, slot, phase):
        js = pl.ds(lo, count)
        both = [j for j in range(lo, lo + count) if j < 2]
        bs = pl.ds(both[0], len(both))
        copies = [
            to_sibling(slot, pw.at[js, 2 + other], rw.at[js, 1]),
            to_sibling(slot + 1, pw.at[bs, other], rw.at[bs, 0]),
            to_sibling(slot + 2, pa.at[js, other], ra.at[js, 0]),
            to_sibling(slot + 3, pa.at[js, 2 + other], ra.at[js, 1]),
        ]
        copies[0].wait_recv()
        for j in range(lo, lo + count):
            rw[j, 1] += pw[j, 2 + core]
            gw[j, 1, r] = rw[j, 1, r]
        for p in row_peers:
            put(rw.at[js, 1, p], gw.at[js, 1, r], F2 + phase, {"row": p})
        copies[1].wait_recv()
        for j in both:
            rw[j, 0] += pw[j, core]
            gw[j, 0, r] = rw[j, 0, r]
        for p in row_peers:
            put(rw.at[bs, 0, p], gw.at[bs, 0, r], F2 + 2 + phase, {"row": p})
        copies[2].wait_recv()
        copies[3].wait_recv()
        for j in range(lo, lo + count):
            hb[2, j] = pa[j, core] + ra[j, 0]
            hb[3, j] = pa[j, 2 + core] + ra[j, 1]
        take(F2 + phase, gw.at[js, 1, pl.ds(0, ROWS - 1)])
        take(F2 + 2 + phase, gw.at[bs, 0, pl.ds(0, ROWS - 1)])
        for j in range(lo, lo + count):
            hb[1, j] = jnp.sum(gw[j, 1], axis=0)
            hb[0, j] = jnp.sum(gw[j, 0], axis=0) if j in both else jnp.zeros((TR, TC), F32)
        for p in z_peers:
            put(hb.at[p, js], kb.at[z_hi, js], F3 + phase, {"cfg": 2 * p + core})
        kb[z_hi, js] = hb[z_hi, js]
        take(F3 + phase, kb.at[pl.ds(0, 3), js])
        for j in range(lo, lo + count):
            chosen = (pat_ref[g, j] + (g == j).astype(jnp.int32)).astype(F32)
            out_ref[:, j, :] = jnp.sum(kb[:, j], axis=0) * chosen

    pw[3, 2] = jnp.zeros((ROWS, TR, TC), F32)
    pw[1, 0] = jnp.zeros((ROWS, TR, TC), F32)
    column(3)
    column(2)
    column(1)
    finish(1, 3, 0, 0)
    take_x(0)
    column(0)
    finish(0, 1, 4, 1)

    for phase, ref in waits:
        pltpu.make_async_copy(ref, ref, send.at[phase]).wait()
    for copy in pairs:
        copy.wait_send()


def local(sigma_above, panels, diag_inverse, pattern, cfg_weight):
    vmem = pl.BlockSpec(memory_space=pltpu.VMEM)
    smem = pl.BlockSpec(memory_space=pltpu.SMEM)
    tiles = [NB - 1 - j for j in range(W)]
    scratch = [pltpu.VMEM((ROWS, 6, TR, TC), F32)]
    scratch += [pltpu.VMEM((COLS, n, TR, TC), F32) for n in tiles]
    scratch += [pltpu.VMEM((ROWS, n, TR, TC), F32) for n in tiles]
    scratch += [pltpu.VMEM((COLS, 4 * TR, 4, TC), F32), pltpu.VMEM((COLS, 3, TR, TC), F32)]
    scratch += [pltpu.VMEM((4 * TR, 4 * FULL), BF16)] * 2
    scratch += [pltpu.VMEM((3, TR, FULL), BF16)] * 2
    scratch += [pltpu.VMEM((6, GROUPS, ROWS, SUB, TC), BF16)] * 2
    scratch += [pltpu.VMEM((n * TR, FULL), BF16) for n in tiles] * 2
    scratch += [pltpu.VMEM((7, GROUPS, ROWS, SUB, TC), BF16)] * 2
    scratch += [pltpu.VMEM((7 * TR, TC), BF16)] * 2
    scratch += [
        pltpu.VMEM((4, 4, ROWS, TR, TC), F32),
        pltpu.VMEM((4, 4, TR, TC), F32),
        pltpu.VMEM((4, 2, ROWS, TR, TC), F32),
        pltpu.VMEM((4, 2, TR, TC), F32),
        pltpu.VMEM((4, 2, ROWS, TR, TC), F32),
        pltpu.VMEM((4, 4, TR, TC), F32),
        pltpu.VMEM((4, 4, TR, TC), F32),
        pltpu.SemaphoreType.DMA((19,)),
        pltpu.SemaphoreType.DMA((19,)),
        pltpu.SemaphoreType.DMA((8,)),
        pltpu.SemaphoreType.DMA((8,)),
    ]
    out = pl.pallas_call(
        kernel,
        name="selected_inverse",
        out_shape=jax.ShapeDtypeStruct((TR, W, TC), F32),
        in_specs=[vmem, vmem, vmem, smem, smem],
        out_specs=vmem,
        scratch_shapes=scratch,
        compiler_params=pltpu.CompilerParams(
            collective_id=0, has_side_effects=True, vmem_limit_bytes=56 << 20
        ),
    )(
        sigma_above.reshape(4 * TR, 4, TC),
        panels.reshape(W, NB, TR, TC),
        diag_inverse.reshape(W, TR, TC),
        pattern,
        cfg_weight,
    )
    return out.reshape(1, GROUPS, 1, SUB, W, TC)


def solution(mesh):
    return jax.shard_map(
        local,
        mesh=mesh,
        in_specs=(
            P("cfg", None, None, "row", None, None, "col"),
            P("cfg", None, None, None, "row", None, "col"),
            P("cfg", None, None, "row", None, "col"),
            P(),
            P("cfg"),
        ),
        out_specs=P("cfg", None, "row", None, None, "col"),
        check_vma=False,
    )
```

time: 948 us -> 137 us (0.14); the launches traced: 937 us -> 136 us
  waiting for transfers between devices: 711 us -> 0 us
  Pallas kernels: 0 us -> 133 us
  local copies, waits for them, and re-layouts: 83 us -> 2.92 us
  blocking collectives: 55.4 us -> 0 us
  matrix products: 28.4 us -> 0 us
  starting transfers between devices: 26 us -> 0 us
  other arithmetic: 18.7 us -> 0 us
  between operations: 14.5 us -> 0.67 us
    unnamed x17 -> x0, waiting for transfers between devices: 669 us -> none
    pallas_call x0 -> x1, Pallas kernels: none -> 133 us  [local(): pl.pallas_call(kernel, name='selected_inverse', out_shape=jax.ShapeDtypeS...]
    all_gather x4 -> x0, blocking collectives: 55.4 us -> none  [local(): gathered = lax.all_gather(panel_tile, 'col', axis=2, tiled=True)]
    reduce_scatter x1 -> x0, waiting for transfers between devices: 38.2 us -> none  [local(): lax.psum_scatter(share_all, 'cfg', scatter_dimension=0, tiled=True)]
    dot_general x8 -> x0, matrix products: 28.4 us -> none  [the longest x4 18.2 us: local(): lax.dot_general(flat_panel, flat_state, (((0,), (0,)), ((), ())), precisi...]
    all_to_all x4 -> x0, starting transfers between devices: 25.5 us -> none  [local(): lax.all_to_all(pieces, ('row', 'col'), split_axis=0, concat_axis=0, tiled...]
    unnamed x40 -> x4, local copies, waits for them, and re-layouts: 24.9 us -> 2.92 us
    transpose x7 -> x0, local copies, waits for them, and re-layouts: 16.8 us -> none  [the longest x4 9.18 us: settle_pieces(): shaped.transpose(2, 1, 4, 0, 3)]
  transfers between devices with their start and end apart: 13 -> 0, of which waited for: 10 -> 0; matrix products, arithmetic and copies ran while one was open for 2% -> 0% of each run, Pallas kernels for 0% -> 0%
where the time goes in v1:
time: 137 us; the launch traced here: 136 us
  Pallas kernels  133 us (97%)
  local copies, waits for them, and re-layouts  2.92 us (2%)
    pallas_call x1, Pallas kernels, local(): pl.pallas_call(kernel, name='selected_inverse', out_shape=jax.ShapeDtypeS...  133 us
    unnamed x4, local copies, waits for them, and re-layouts  2.92 us

profile of v1, /device:TPU:6, one launch (start us, length us, event | category | flops | bytes accessed | tf_op | source)
XLA Modules:
  0.0 136.4 jit_solution(3278518586322037687)
XLA Ops:
  0.7 0.0 copy-start
  0.7 0.7 copy-done
  1.3 0.7 copy.6.pat_ref
  2.0 132.8 %selected_inverse.1 = f32[64,4,128]{2,1,0:T(4,128)} custom-call(f32[256,4,128]{2,1,0:T(4,128)} %bitcast.7, f32[4,8,64,128]{3,2,1,0:T(8,128)} %bitcast.6, f32[4,64,128]{2,1,0:T(8,128)} %bitcast.9, s32[8,4]{1,0:T(8,128)} %copy.6.pat_ref, f32[1]{0:T(128)S(6)} %copy.9.w_ref), custom_call_target="tpu_custom_call" | custom-call | tf_op jit(solution)/shard_map/selected_inverse/pallas_call | solution.py:294
  134.8 1.6 %copy.10 = f32[1,4,1,16,4,128]{5,4,3,2,1,0:T(4,128)} copy(f32[1,4,1,16,4,128]{5,4,3,2,1,0:T(4,128)} %bitcast.8) | data formatting | bytes 262144
Async XLA Ops:
  0.7 0.7 copy-start

commit v2 on v1

v2 whole, which is shorter than its diff:
```python
import jax
import jax.numpy as jnp
from jax import lax
from jax.experimental import pallas as pl
from jax.experimental.pallas import tpu as pltpu
from jax.sharding import PartitionSpec as P

MESH = pl.DeviceIdType.MESH
F32 = jnp.float32
BF16 = jnp.bfloat16
W = 4
NB = 8
ROWS = 8
COLS = 4
GROUPS = 4
SUB = 16
TR = 64
TC = 128
FULL = 512
WINDOW_BLOCKS = ((3, 2), (3, 1), (2, 1), (3, 0), (2, 0), (1, 0))
WINDOW_PHASES = ((0, 1), (1, 2), (3, 3))
WINDOW_LATER = {1: (0, 1), 0: (1, 2)}


def split(x):
    hi = x.astype(BF16)
    return hi, (x - hi.astype(F32)).astype(BF16)


def dot3(ah, al, bh, bl, dims=(((1,), (0,)), ((), ()))):
    def one(a, b):
        return lax.dot_general(a, b, dims, preferred_element_type=F32)

    return one(ah, bh) + (one(ah, bl) + one(al, bh))


def kernel(
    a_ref, u_ref, d_ref, pat_ref, w_ref, out_ref,
    tr, zx0, zx1, zx2, zx3, zr, zw, az, ax, dg, qs, qr,
    ah, al, dh, dl, th, tl, zh0, zh1, zh2, zh3, zl0, zl1, zl2, zl3, bh, bl, wh, wl, qh, ql,
    pw, pa, rw, ra, gw, hb, kb,
    send, recv, send1, recv1,
):
    zx = (zx0, zx1, zx2, zx3)
    zh, zl = (zh0, zh1, zh2, zh3), (zl0, zl1, zl2, zl3)
    g, r, c = lax.axis_index("cfg"), lax.axis_index("row"), lax.axis_index("col")
    z_hi, core = lax.div(g, 2), lax.rem(g, 2)
    y, z = lax.div(r, 2), lax.rem(r, 2)
    other = 1 - core
    row_peers = [lax.rem(r + d, ROWS) for d in range(1, ROWS)]
    y_peers = [2 * lax.rem(y + d, 4) + z for d in range(1, 4)]
    z_peer = {"row": 2 * y + 1 - z}
    right, left = lax.rem(c + 1, COLS), lax.rem(c + 3, COLS)
    col_peers = [lax.rem(c + d, COLS) for d in range(1, COLS)]
    z_peers = [lax.rem(z_hi + d, 4) for d in range(1, 4)]
    sibling = {"cfg": 2 * z_hi + other}

    barrier = pltpu.get_barrier_semaphore()
    everyone = [{"row": p} for p in row_peers] + [{"col": p} for p in col_peers]
    everyone += [{"cfg": 2 * p + core} for p in z_peers] + [sibling]
    for peer in everyone:
        pl.semaphore_signal(barrier, inc=1, device_id=peer, device_id_type=MESH)
    pl.semaphore_wait(barrier, len(everyone))

    waits = []

    def put(src, dst, phase, peer):
        pltpu.make_async_remote_copy(
            src_ref=src, dst_ref=dst, send_sem=send.at[phase], recv_sem=recv.at[phase],
            device_id=peer, device_id_type=MESH,
        ).start()

    def take(phase, ref):
        pltpu.make_async_copy(ref, ref, recv.at[phase]).wait()
        waits.append((phase, ref))

    def over_rows(src, dst, phase):
        for p in row_peers:
            put(src, dst, phase, {"row": p})

    def over_cols(src, dst, phase):
        for p in col_peers:
            put(src, dst, phase, {"col": p})

    X, R, T, D, F2, F3, WZ, Q, AZ, AR, AL, RR, RL = 0, 4, 8, 11, 12, 18, 21, 23, 27, 28, 30, 32, 33

    def panel(k, j):
        return u_ref[j, k] * pat_ref[j, k].astype(F32)

    def send_z(j):
        over_cols(zx[j].at[c], zx[j].at[c], X + j)
        above = zx[j].at[c, pl.ds(NB - 5 - j, 4)]
        for p in y_peers:
            put(above, zr.at[j, y], R + j, {"row": p})
        for m in range(4):
            zr[j, y, m] = zx[j][c, NB - 5 - j + m]

    def send_w(j):
        slot, count = WINDOW_LATER[j]
        for m in range(count):
            zw[r, slot + m] = zx[j][c, 1 + m]
        piece = zw.at[r, pl.ds(slot, count)]
        over_rows(piece, piece, WZ + j)

    def take_w(j):
        slot, count = WINDOW_LATER[j]
        take(WZ + j, zw.at[pl.ds(0, ROWS - 1), pl.ds(slot, count)])
        for m in range(slot, slot + count):
            for q in range(ROWS):
                hi, lo = split(zw[q, m].reshape(GROUPS, SUB, TC))
                wh[m, :, q] = hi
                wl[m, :, q] = lo

    def take_x(j):
        take(X + j, zx[j].at[pl.ds(0, COLS - 1)])
        for q in range(COLS):
            hi, lo = split(zx[j][q].reshape(-1, TC))
            zh[j][:, q * TC:(q + 1) * TC] = hi
            zl[j][:, q * TC:(q + 1) * TC] = lo

    def take_t(phase):
        first, count = WINDOW_PHASES[phase]
        take(T + phase, tr.at[pl.ds(0, ROWS - 1), pl.ds(first, count)])
        for s in range(first, first + count):
            for q in range(ROWS):
                hi, lo = split(tr[q, s].reshape(GROUPS, SUB, TC))
                th[s, :, q] = hi
                tl[s, :, q] = lo

    def send_t(phase):
        first, count = WINDOW_PHASES[phase]
        for s in range(first, first + count):
            tr[r, s] = panel(*WINDOW_BLOCKS[s])
        piece = tr.at[r, pl.ds(first, count)]
        over_rows(piece, piece, T + phase)

    for m in range(4):
        zx[3][c, m] = -panel(W + m, 3)
    send_z(3)
    for phase in range(3):
        send_t(phase)

    source = lax.broadcasted_iota(jnp.int32, (2 * TC, 2 * TC), 0)
    target = lax.broadcasted_iota(jnp.int32, (2 * TC, 2 * TC), 1)
    parity = lax.rem(lax.div(source, SUB), 2)
    place = parity * TC + lax.div(source, 2 * SUB) * SUB + lax.rem(source, SUB)
    regroup = (place == target).astype(F32).astype(BF16)
    for pair in range(2):
        both = jnp.concatenate([a_ref[:, 2 * pair, :], a_ref[:, 2 * pair + 1, :]], axis=1)
        hi = both.astype(BF16)
        rest = both - hi.astype(F32)
        mid = rest.astype(BF16)
        low = (rest - mid.astype(F32)).astype(BF16)
        out = (
            jnp.dot(hi, regroup, preferred_element_type=F32)
            + jnp.dot(mid, regroup, preferred_element_type=F32)
            + jnp.dot(low, regroup, preferred_element_type=F32)
        )
        az[0, pair] = out[:, :TC]
        az[1, pair] = out[:, TC:]
    put(az.at[1 - z], ax.at[c, z], AZ, z_peer)
    ax[c, z] = az[z]

    def send_a(part, half):
        piece = ax.at[c, half]
        put(piece, piece, AR + part, {"col": right})
        put(piece, piece, AL + part, {"col": left})

    send_a(0, z)
    for k in range(1, W):
        dg[c, k - 1] = d_ref[k]

    def relay_right():
        take(AR, ax.at[left, z])
        put(ax.at[left, z], ax.at[left, z], RR, {"col": right})

    def relay_left():
        take(AL + 1, ax.at[right, 1 - z])
        put(ax.at[right, 1 - z], ax.at[right, 1 - z], RL, {"col": left})

    def minus_product(acc, i, j):
        s = WINDOW_BLOCKS.index((i, j))
        part = dot3(
            zh[i][...], zl[i][...], th[s].reshape(FULL, TC), tl[s].reshape(FULL, TC)
        ).reshape(NB - 1 - i, TR, TC)
        for k in range(i + 1, NB):
            acc[k - j - 1] -= part[k - i - 1]

    for j in (2, 1, 0):
        take_t(2 - j)
        acc = [-panel(k, j) for k in range(j + 1, NB)]
        for i in range(W - 1, j + 1, -1):
            minus_product(acc, i, j)
        take_x(j + 1)
        minus_product(acc, j + 1, j)
        for m in range(NB - 1 - j):
            zx[j][c, m] = acc[m]
        send_z(j)
        if j < 2:
            send_w(j)
        if j == 2:
            take(AZ, ax.at[c, 1 - z])
            send_a(1, 1 - z)
            relay_right()
        if j == 1:
            over_cols(dg.at[c], dg.at[c], D)
            relay_left()

    take(AR + 1, ax.at[left, 1 - z])
    take(AL, ax.at[right, z])
    take(RR, ax.at[0, 0])
    take(RL, ax.at[0, 1])
    for q in range(COLS):
        for p in range(2):
            for m in range(2):
                hi, lo = split(ax[q, m, p])
                lanes = slice((2 * q + p) * TC, (2 * q + p + 1) * TC)
                ah[m * 4 * TR:(m + 1) * 4 * TR, lanes] = hi
                al[m * 4 * TR:(m + 1) * 4 * TR, lanes] = lo
    take(D, dg.at[pl.ds(0, COLS - 1)])
    for q in range(COLS):
        for k in range(3):
            hi, lo = split(dg[q, k])
            dh[k, :, q * TC:(q + 1) * TC] = hi
            dl[k, :, q * TC:(q + 1) * TC] = lo

    weight = w_ref[0]

    def half_column(j):
        take(R + j, zr.at[j, pl.ds(0, 3)])
        for q in range(4):
            for m in range(4):
                hi, lo = split(zr[j, q, m].reshape(GROUPS, SUB, TC))
                bh[:, m, q] = hi
                bl[:, m, q] = lo
        part = weight * dot3(
            ah[...], al[...], bh[...].reshape(2 * FULL, TC), bl[...].reshape(2 * FULL, TC)
        )
        qs[j, 0] = part[:4 * TR]
        qs[j, 1] = part[4 * TR:]
        put(qs.at[j, 1 - z], qr.at[j], Q + j, z_peer)

    def column(j):
        blocks = NB - 1 - j
        first = blocks - 4
        take(Q + j, qr.at[j])
        q_above = qs[j, z] + qr[j]
        hi, lo = split(q_above)
        qh[first * TR:blocks * TR, :] = hi
        ql[first * TR:blocks * TR, :] = lo
        q_above = q_above.reshape(4, TR, TC)
        for m in range(4):
            pa[j, m] = q_above[m]
        inside = []
        for m in range(first):
            k = j + 1 + m
            if m == 0:
                s = WINDOW_BLOCKS.index((k, j))
                q_in = -weight * dot3(
                    dh[k - 1], dl[k - 1], th[s].reshape(FULL, TC), tl[s].reshape(FULL, TC)
                )
            else:
                s = WINDOW_LATER[j][0] + m - 1
                q_in = weight * dot3(
                    dh[k - 1], dl[k - 1], wh[s].reshape(FULL, TC), wl[s].reshape(FULL, TC)
                )
            hi, lo = split(q_in)
            qh[m * TR:(m + 1) * TR, :] = hi
            ql[m * TR:(m + 1) * TR, :] = lo
            inside.append(q_in)
        for l in range(j, W):
            start = (l - j) * TR
            part = dot3(
                zh[l][...], zl[l][...],
                qh[start:blocks * TR, :], ql[start:blocks * TR, :],
                (((0,), (0,)), ((), ())),
            ).reshape(GROUPS, ROWS, SUB, TC)
            for q in range(ROWS):
                pw[j, l, q] = part[:, q].reshape(TR, TC)
            pw[j, l, r] += weight * d_ref[j] if l == j else inside[l - j - 1]

    pairs = []

    def to_sibling(slot, src, dst):
        copy = pltpu.make_async_remote_copy(
            src_ref=src, dst_ref=dst, send_sem=send1.at[slot], recv_sem=recv1.at[slot],
            device_id=sibling, device_id_type=MESH,
        )
        copy.start()
        pairs.append(copy)
        return copy

    def finish(lo, count, phase):
        js = pl.ds(lo, count)
        columns = range(lo, lo + count)
        both = [j for j in columns if j < 2]
        bs = pl.ds(lo, len(both))
        copies = [
            to_sibling(4 * phase, pw.at[js, 2 + other], rw.at[js, 1]),
            to_sibling(4 * phase + 1, pa.at[js, other], ra.at[js, 0]),
            to_sibling(4 * phase + 2, pa.at[js, 2 + other], ra.at[js, 1]),
        ]
        if both:
            copies.append(to_sibling(4 * phase + 3, pw.at[bs, other], rw.at[bs, 0]))
        yield
        copies[0].wait_recv()
        for j in columns:
            rw[j, 1] += pw[j, 2 + core]
            gw[j, 1, r] = rw[j, 1, r]
        for p in row_peers:
            put(rw.at[js, 1, p], gw.at[js, 1, r], F2 + 2 * phase, {"row": p})
        if both:
            copies[3].wait_recv()
            for j in both:
                rw[j, 0] += pw[j, core]
                gw[j, 0, r] = rw[j, 0, r]
            for p in row_peers:
                put(rw.at[bs, 0, p], gw.at[bs, 0, r], F2 + 2 * phase + 1, {"row": p})
        copies[1].wait_recv()
        copies[2].wait_recv()
        for j in columns:
            hb[2, j] = pa[j, core] + ra[j, 0]
            hb[3, j] = pa[j, 2 + core] + ra[j, 1]
        for p in z_peers:
            @pl.when(p >= 2)
            def _():
                put(hb.at[p, js], kb.at[z_hi, js], F3 + phase, {"cfg": 2 * p + core})
        yield
        take(F2 + 2 * phase, gw.at[js, 1, pl.ds(0, ROWS - 1)])
        if both:
            take(F2 + 2 * phase + 1, gw.at[bs, 0, pl.ds(0, ROWS - 1)])
        for j in columns:
            hb[1, j] = jnp.sum(gw[j, 1], axis=0)
            hb[0, j] = jnp.sum(gw[j, 0], axis=0) if j in both else jnp.zeros((TR, TC), F32)
        for p in z_peers:
            @pl.when(p < 2)
            def _():
                put(hb.at[p, js], kb.at[z_hi, js], F3 + phase, {"cfg": 2 * p + core})
        kb[z_hi, js] = hb[z_hi, js]
        yield
        take(F3 + phase, kb.at[pl.ds(0, 3), js])
        for j in columns:
            chosen = (pat_ref[j, g] + (g == j).astype(jnp.int32)).astype(F32)
            out_ref[:, j, :] = jnp.sum(kb[:, j], axis=0) * chosen
        yield

    pw[3, 2] = jnp.zeros((ROWS, TR, TC), F32)
    pw[1, 0] = jnp.zeros((ROWS, TR, TC), F32)
    half_column(3)
    half_column(2)
    half_column(1)
    column(3)
    column(2)
    first = finish(2, 2, 0)
    next(first)
    take_w(1)
    column(1)
    second = finish(1, 1, 1)
    next(second)
    next(first)
    half_column(0)
    next(second)
    take_w(0)
    take_x(0)
    column(0)
    third = finish(0, 1, 2)
    next(third)
    next(first)
    next(second)
    next(third)
    next(third)
    next(first)
    next(second)
    next(third)

    for phase, ref in waits:
        pltpu.make_async_copy(ref, ref, send.at[phase]).wait()
    for copy in pairs:
        copy.wait_send()


def local(sigma_above, panels, diag_inverse, pattern, cfg_weight):
    vmem = pl.BlockSpec(memory_space=pltpu.VMEM)
    smem = pl.BlockSpec(memory_space=pltpu.SMEM)
    tiles = [NB - 1 - j for j in range(W)]
    scratch = [pltpu.VMEM((ROWS, 6, TR, TC), F32)]
    scratch += [pltpu.VMEM((COLS, n, TR, TC), F32) for n in tiles]
    scratch += [pltpu.VMEM((W, 4, 4, TR, TC), F32), pltpu.VMEM((ROWS, 3, TR, TC), F32)]
    scratch += [pltpu.VMEM((2, 2, 4 * TR, TC), F32), pltpu.VMEM((COLS, 2, 2, 4 * TR, TC), F32)]
    scratch += [pltpu.VMEM((COLS, 3, TR, TC), F32)]
    scratch += [pltpu.VMEM((W, 2, 4 * TR, TC), F32), pltpu.VMEM((W, 4 * TR, TC), F32)]
    scratch += [pltpu.VMEM((8 * TR, 2 * FULL), BF16)] * 2
    scratch += [pltpu.VMEM((3, TR, FULL), BF16)] * 2
    scratch += [pltpu.VMEM((6, GROUPS, ROWS, SUB, TC), BF16)] * 2
    scratch += [pltpu.VMEM((n * TR, FULL), BF16) for n in tiles] * 2
    scratch += [pltpu.VMEM((GROUPS, 4, 4, SUB, TC), BF16)] * 2
    scratch += [pltpu.VMEM((3, GROUPS, ROWS, SUB, TC), BF16)] * 2
    scratch += [pltpu.VMEM((7 * TR, TC), BF16)] * 2
    scratch += [
        pltpu.VMEM((4, 4, ROWS, TR, TC), F32),
        pltpu.VMEM((4, 4, TR, TC), F32),
        pltpu.VMEM((4, 2, ROWS, TR, TC), F32),
        pltpu.VMEM((4, 2, TR, TC), F32),
        pltpu.VMEM((4, 2, ROWS, TR, TC), F32),
        pltpu.VMEM((4, 4, TR, TC), F32),
        pltpu.VMEM((4, 4, TR, TC), F32),
        pltpu.SemaphoreType.DMA((34,)),
        pltpu.SemaphoreType.DMA((34,)),
        pltpu.SemaphoreType.DMA((12,)),
        pltpu.SemaphoreType.DMA((12,)),
    ]
    out = pl.pallas_call(
        kernel,
        name="selected_inverse",
        out_shape=jax.ShapeDtypeStruct((TR, W, TC), F32),
        in_specs=[vmem, vmem, vmem, smem, smem],
        out_specs=vmem,
        scratch_shapes=scratch,
        compiler_params=pltpu.CompilerParams(
            collective_id=0, has_side_effects=True, vmem_limit_bytes=56 << 20
        ),
    )(
        sigma_above.reshape(4 * TR, 4, TC),
        panels.reshape(W, NB, TR, TC),
        diag_inverse.reshape(W, TR, TC),
        pattern.T,
        cfg_weight,
    )
    return out.reshape(1, GROUPS, 1, SUB, W, TC)


def solution(mesh):
    return jax.shard_map(
        local,
        mesh=mesh,
        in_specs=(
            P("cfg", None, None, "row", None, None, "col"),
            P("cfg", None, None, None, "row", None, "col"),
            P("cfg", None, None, "row", None, "col"),
            P(),
            P("cfg"),
        ),
        out_specs=P("cfg", None, "row", None, None, "col"),
        check_vma=False,
    )
```

time: 137 us -> 117 us (0.85)
  Pallas kernels: 133 us -> 114 us
    pallas_call x1, Pallas kernels: 133 us -> 114 us  [local(): pl.pallas_call(kernel, name='selected_inverse', out_shape=jax.ShapeDtypeS...]
    unnamed x4 -> x1, local copies, waits for them, and re-layouts: 2.92 us -> 1.57 us
where the time goes in v2:
time: 117 us
  Pallas kernels  114 us (97%)
  local copies, waits for them, and re-layouts  1.57 us (1%)
    pallas_call x1, Pallas kernels, local(): pl.pallas_call(kernel, name='selected_inverse', out_shape=jax.ShapeDtypeS...  114 us

profile of v2, /device:TPU:6, one launch (start us, length us, event | category | flops | bytes accessed | tf_op | source)
XLA Modules:
  0.0 116.5 jit_solution(4321830026763405724)
XLA Ops:
  0.7 114.3 %selected_inverse.1 = f32[64,4,128]{2,1,0:T(4,128)} custom-call(f32[256,4,128]{2,1,0:T(4,128)} %bitcast.8, f32[4,8,64,128]{3,2,1,0:T(8,128)} %bitcast.7, f32[4,64,128]{2,1,0:T(8,128)} %bitcast.10, s32[4,8]{1,0:T(4,128)} %bitcast.11, f32[1]{0:T(128)S(6)} %copy.8.w_ref), custom_call_target="tpu_custom_call" | custom-call | tf_op jit(solution)/shard_map/selected_inverse/pallas_call | solution.py:412
  115.0 1.6 %copy.9 = f32[1,4,1,16,4,128]{5,4,3,2,1,0:T(4,128)} copy(f32[1,4,1,16,4,128]{5,4,3,2,1,0:T(4,128)} %bitcast.9) | data formatting | bytes 262144

commit v3 on v2

--- a/solution.py
+++ b/solution.py
@@ -50,7 +50,6 @@
     row_peers = [lax.rem(r + d, ROWS) for d in range(1, ROWS)]
     y_peers = [2 * lax.rem(y + d, 4) + z for d in range(1, 4)]
     z_peer = {"row": 2 * y + 1 - z}
-    right, left = lax.rem(c + 1, COLS), lax.rem(c + 3, COLS)
     col_peers = [lax.rem(c + d, COLS) for d in range(1, COLS)]
     z_peers = [lax.rem(z_hi + d, 4) for d in range(1, 4)]
     sibling = {"cfg": 2 * z_hi + other}
@@ -63,6 +62,13 @@
     pl.semaphore_wait(barrier, len(everyone))
 
     waits = []
+    later_waits = []
+
+    def when(condition, action):
+        if condition is None:
+            action()
+        else:
+            pl.when(condition)(action)
 
     def put(src, dst, phase, peer):
         pltpu.make_async_remote_copy(
@@ -82,18 +88,19 @@
         for p in col_peers:
             put(src, dst, phase, {"col": p})
 
-    X, R, T, D, F2, F3, WZ, Q, AZ, AR, AL, RR, RL = 0, 4, 8, 11, 12, 18, 21, 23, 27, 28, 30, 32, 33
+    X, R, T, D, F2, F3, WZ, Q, AZ, A = 0, 4, 8, 11, 12, 20, 24, 26, 30, 31
 
     def panel(k, j):
         return u_ref[j, k] * pat_ref[j, k].astype(F32)
 
-    def send_z(j):
+    def send_x(j):
         over_cols(zx[j].at[c], zx[j].at[c], X + j)
-        above = zx[j].at[c, pl.ds(NB - 5 - j, 4)]
-        for p in y_peers:
-            put(above, zr.at[j, y], R + j, {"row": p})
+
+    def send_y(j):
         for m in range(4):
             zr[j, y, m] = zx[j][c, NB - 5 - j + m]
+        for p in y_peers:
+            put(zr.at[j, y], zr.at[j, y], R + j, {"row": p})
 
     def send_w(j):
         slot, count = WINDOW_LATER[j]
@@ -134,11 +141,12 @@
         piece = tr.at[r, pl.ds(first, count)]
         over_rows(piece, piece, T + phase)
 
+    send_t(0)
     for m in range(4):
         zx[3][c, m] = -panel(W + m, 3)
-    send_z(3)
-    for phase in range(3):
-        send_t(phase)
+    send_x(3)
+    send_t(1)
+    send_t(2)
 
     source = lax.broadcasted_iota(jnp.int32, (2 * TC, 2 * TC), 0)
     target = lax.broadcasted_iota(jnp.int32, (2 * TC, 2 * TC), 1)
@@ -161,22 +169,31 @@
     put(az.at[1 - z], ax.at[c, z], AZ, z_peer)
     ax[c, z] = az[z]
 
-    def send_a(part, half):
-        piece = ax.at[c, half]
-        put(piece, piece, AR + part, {"col": right})
-        put(piece, piece, AL + part, {"col": left})
-
-    send_a(0, z)
     for k in range(1, W):
         dg[c, k - 1] = d_ref[k]
 
-    def relay_right():
-        take(AR, ax.at[left, z])
-        put(ax.at[left, z], ax.at[left, z], RR, {"col": right})
-
-    def relay_left():
-        take(AL + 1, ax.at[right, 1 - z])
-        put(ax.at[right, 1 - z], ax.at[right, 1 - z], RL, {"col": left})
+    parts = ((z, 0), (z, 1), (1 - z, 0), (1 - z, 1))
+
+    def send_a(part):
+        piece = ax.at[(c, *parts[part])]
+        over_cols(piece, piece, A + part)
+
+    def take_a(part):
+        half, pair = parts[part]
+        take(A + part, ax.at[pl.ds(0, COLS - 1), half, pair])
+        for q in range(COLS):
+            hi, lo = split(ax[q, half, pair])
+            lanes = slice((2 * q + pair) * TC, (2 * q + pair + 1) * TC)
+            ah[half, :, lanes] = hi
+            al[half, :, lanes] = lo
+
+    def take_d():
+        take(D, dg.at[pl.ds(0, COLS - 1)])
+        for q in range(COLS):
+            for k in range(3):
+                hi, lo = split(dg[q, k])
+                dh[k, :, q * TC:(q + 1) * TC] = hi
+                dl[k, :, q * TC:(q + 1) * TC] = lo
 
     def minus_product(acc, i, j):
         s = WINDOW_BLOCKS.index((i, j))
@@ -186,45 +203,24 @@
         for k in range(i + 1, NB):
             acc[k - j - 1] -= part[k - i - 1]
 
-    for j in (2, 1, 0):
-        take_t(2 - j)
-        acc = [-panel(k, j) for k in range(j + 1, NB)]
-        for i in range(W - 1, j + 1, -1):
-            minus_product(acc, i, j)
-        take_x(j + 1)
-        minus_product(acc, j + 1, j)
-        for m in range(NB - 1 - j):
-            zx[j][c, m] = acc[m]
-        send_z(j)
-        if j < 2:
-            send_w(j)
-        if j == 2:
-            take(AZ, ax.at[c, 1 - z])
-            send_a(1, 1 - z)
-            relay_right()
-        if j == 1:
-            over_cols(dg.at[c], dg.at[c], D)
-            relay_left()
-
-    take(AR + 1, ax.at[left, 1 - z])
-    take(AL, ax.at[right, z])
-    take(RR, ax.at[0, 0])
-    take(RL, ax.at[0, 1])
-    for q in range(COLS):
-        for p in range(2):
-            for m in range(2):
-                hi, lo = split(ax[q, m, p])
-                lanes = slice((2 * q + p) * TC, (2 * q + p + 1) * TC)
-                ah[m * 4 * TR:(m + 1) * 4 * TR, lanes] = hi
-                al[m * 4 * TR:(m + 1) * 4 * TR, lanes] = lo
-    take(D, dg.at[pl.ds(0, COLS - 1)])
-    for q in range(COLS):
-        for k in range(3):
-            hi, lo = split(dg[q, k])
-            dh[k, :, q * TC:(q + 1) * TC] = hi
-            dl[k, :, q * TC:(q + 1) * TC] = lo
+    send_a(0)
+    send_a(1)
+    send_y(3)
 
     weight = w_ref[0]
+
+    pairs = []
+
+    def to_sibling(slot, src, dst):
+        copy = pltpu.make_async_remote_copy(
+            src_ref=src, dst_ref=dst, send_sem=send1.at[slot], recv_sem=recv1.at[slot],
+            device_id=sibling, device_id_type=MESH,
+        )
+        copy.start()
+        pairs.append(copy)
+        return copy
+
+    above = {}
 
     def half_column(j):
         take(R + j, zr.at[j, pl.ds(0, 3)])
@@ -234,7 +230,7 @@
                 bh[:, m, q] = hi
                 bl[:, m, q] = lo
         part = weight * dot3(
-            ah[...], al[...], bh[...].reshape(2 * FULL, TC), bl[...].reshape(2 * FULL, TC)
+            ah[...].reshape(8 * TR, 2 * FULL), al[...].reshape(8 * TR, 2 * FULL), bh[...].reshape(2 * FULL, TC), bl[...].reshape(2 * FULL, TC)
         )
         qs[j, 0] = part[:4 * TR]
         qs[j, 1] = part[4 * TR:]
@@ -251,6 +247,9 @@
         q_above = q_above.reshape(4, TR, TC)
         for m in range(4):
             pa[j, m] = q_above[m]
+        above[j] = [
+            to_sibling(4 * j + t, pa.at[j, 2 * t + other], ra.at[j, t]) for t in range(2)
+        ]
         inside = []
         for m in range(first):
             k = j + 1 + m
@@ -279,104 +278,147 @@
                 pw[j, l, q] = part[:, q].reshape(TR, TC)
             pw[j, l, r] += weight * d_ref[j] if l == j else inside[l - j - 1]
 
-    pairs = []
-
-    def to_sibling(slot, src, dst):
-        copy = pltpu.make_async_remote_copy(
-            src_ref=src, dst_ref=dst, send_sem=send1.at[slot], recv_sem=recv1.at[slot],
-            device_id=sibling, device_id_type=MESH,
-        )
-        copy.start()
-        pairs.append(copy)
-        return copy
-
-    def finish(lo, count, phase):
-        js = pl.ds(lo, count)
-        columns = range(lo, lo + count)
-        both = [j for j in columns if j < 2]
-        bs = pl.ds(lo, len(both))
-        copies = [
-            to_sibling(4 * phase, pw.at[js, 2 + other], rw.at[js, 1]),
-            to_sibling(4 * phase + 1, pa.at[js, other], ra.at[js, 0]),
-            to_sibling(4 * phase + 2, pa.at[js, 2 + other], ra.at[js, 1]),
-        ]
-        if both:
-            copies.append(to_sibling(4 * phase + 3, pw.at[bs, other], rw.at[bs, 0]))
+    def finish(j):
+        slots = [1, 0] if j < 2 else [1]
+        used = {t: None if 2 * t >= j else core == 1 for t in slots}
+        unused = {t: None if 2 * t >= j else core == 0 for t in slots}
+        copies = {}
+        for t in slots:
+            copies[t] = pltpu.make_async_remote_copy(
+                src_ref=pw.at[j, 2 * t + other], dst_ref=rw.at[j, t],
+                send_sem=send1.at[4 * j + 2 + t], recv_sem=recv1.at[4 * j + 2 + t],
+                device_id=sibling, device_id_type=MESH,
+            )
+            when(unused[t], copies[t].start)
+            later_waits.append((unused[t], copies[t].wait_send))
         yield
-        copies[0].wait_recv()
-        for j in columns:
-            rw[j, 1] += pw[j, 2 + core]
-            gw[j, 1, r] = rw[j, 1, r]
-        for p in row_peers:
-            put(rw.at[js, 1, p], gw.at[js, 1, r], F2 + 2 * phase, {"row": p})
-        if both:
-            copies[3].wait_recv()
-            for j in both:
-                rw[j, 0] += pw[j, core]
-                gw[j, 0, r] = rw[j, 0, r]
-            for p in row_peers:
-                put(rw.at[bs, 0, p], gw.at[bs, 0, r], F2 + 2 * phase + 1, {"row": p})
-        copies[1].wait_recv()
-        copies[2].wait_recv()
-        for j in columns:
-            hb[2, j] = pa[j, core] + ra[j, 0]
-            hb[3, j] = pa[j, 2 + core] + ra[j, 1]
-        for p in z_peers:
-            @pl.when(p >= 2)
-            def _():
-                put(hb.at[p, js], kb.at[z_hi, js], F3 + phase, {"cfg": 2 * p + core})
+        for t in slots:
+            def add(t=t):
+                copies[t].wait_recv()
+                rw[j, t] += pw[j, 2 * t + core]
+                gw[j, t, r] = rw[j, t, r]
+                for p in row_peers:
+                    put(rw.at[j, t, p], gw.at[j, t, r], F2 + 2 * j + t, {"row": p})
+
+            when(used[t], add)
+        for t, copy in enumerate(above[j]):
+            copy.wait_recv()
+            hb[2 + t, j] = pa[j, 2 * t + core] + ra[j, t]
+        send_out(j, 2)
+        send_out(j, 3)
         yield
-        take(F2 + 2 * phase, gw.at[js, 1, pl.ds(0, ROWS - 1)])
-        if both:
-            take(F2 + 2 * phase + 1, gw.at[bs, 0, pl.ds(0, ROWS - 1)])
-        for j in columns:
-            hb[1, j] = jnp.sum(gw[j, 1], axis=0)
-            hb[0, j] = jnp.sum(gw[j, 0], axis=0) if j in both else jnp.zeros((TR, TC), F32)
-        for p in z_peers:
-            @pl.when(p < 2)
-            def _():
-                put(hb.at[p, js], kb.at[z_hi, js], F3 + phase, {"cfg": 2 * p + core})
-        kb[z_hi, js] = hb[z_hi, js]
+        for t in slots:
+            def total(t=t):
+                piece = gw.at[j, t, pl.ds(0, ROWS - 1)]
+                pltpu.make_async_copy(piece, piece, recv.at[F2 + 2 * j + t]).wait()
+                hb[t, j] = jnp.sum(gw[j, t], axis=0)
+
+            def sent(t=t):
+                piece = gw.at[j, t, pl.ds(0, ROWS - 1)]
+                pltpu.make_async_copy(piece, piece, send.at[F2 + 2 * j + t]).wait()
+
+            when(used[t], total)
+            later_waits.append((used[t], sent))
+            send_out(j, t)
+        kb[z_hi, j] = hb[z_hi, j]
         yield
-        take(F3 + phase, kb.at[pl.ds(0, 3), js])
-        for j in columns:
+        l = 2 * z_hi + core
+
+        @pl.when(l >= j)
+        def _():
+            piece = kb.at[pl.ds(0, 3), j]
+            pltpu.make_async_copy(piece, piece, recv.at[F3 + j]).wait()
             chosen = (pat_ref[j, g] + (g == j).astype(jnp.int32)).astype(F32)
             out_ref[:, j, :] = jnp.sum(kb[:, j], axis=0) * chosen
+
+        if j > 0:
+            @pl.when(l < j)
+            def _():
+                out_ref[:, j, :] = jnp.zeros((TR, TC), F32)
         yield
 
-    pw[3, 2] = jnp.zeros((ROWS, TR, TC), F32)
-    pw[1, 0] = jnp.zeros((ROWS, TR, TC), F32)
-    half_column(3)
-    half_column(2)
+    def send_out(j, t):
+        condition = z_hi != t
+        if 2 * t < j:
+            condition = jnp.logical_and(condition, core == 1)
+
+        def copy():
+            return pltpu.make_async_remote_copy(
+                src_ref=hb.at[t, j], dst_ref=kb.at[z_hi, j], send_sem=send.at[F3 + j],
+                recv_sem=recv.at[F3 + j], device_id={"cfg": 2 * t + core}, device_id_type=MESH,
+            )
+
+        when(condition, lambda: copy().start())
+        later_waits.append((condition, lambda: copy().wait_send()))
+
+    hb[0:2] = jnp.zeros((2, 4, TR, TC), F32)
+    for j in (2, 1, 0):
+        take_t(2 - j)
+        acc = [-panel(k, j) for k in range(j + 1, NB)]
+        for i in range(W - 1, j + 1, -1):
+            minus_product(acc, i, j)
+        if j == 1:
+            take_a(0)
+            take_a(1)
+        if j == 0:
+            take_a(2)
+            take_a(3)
+            half_column(3)
+            half_column(2)
+        take_x(j + 1)
+        minus_product(acc, j + 1, j)
+        for m in range(NB - 1 - j):
+            zx[j][c, m] = acc[m]
+        if j > 0:
+            send_x(j)
+        send_y(j)
+        if j < 2:
+            send_w(j)
+        if j == 2:
+            take(AZ, ax.at[c, 1 - z])
+            send_a(2)
+            send_a(3)
+        if j == 1:
+            over_cols(dg.at[c], dg.at[c], D)
+        if j == 0:
+            send_x(0)
+
+    column(3)
+    steps = {3: finish(3)}
+    next(steps[3])
+    take_d()
+    column(2)
+    steps[2] = finish(2)
+    next(steps[2])
+    next(steps[3])
     half_column(1)
-    column(3)
-    column(2)
-    first = finish(2, 2, 0)
-    next(first)
     take_w(1)
+    next(steps[2])
     column(1)
-    second = finish(1, 1, 1)
-    next(second)
-    next(first)
+    steps[1] = finish(1)
+    next(steps[1])
+    next(steps[3])
+    next(steps[1])
     half_column(0)
-    next(second)
+    next(steps[2])
     take_w(0)
     take_x(0)
     column(0)
-    third = finish(0, 1, 2)
-    next(third)
-    next(first)
-    next(second)
-    next(third)
-    next(third)
-    next(first)
-    next(second)
-    next(third)
+    steps[0] = finish(0)
+    next(steps[0])
+    next(steps[1])
+    next(steps[0])
+    for j in (3, 2, 1):
+        next(steps[j])
+    next(steps[0])
+    next(steps[0])
 
     for phase, ref in waits:
         pltpu.make_async_copy(ref, ref, send.at[phase]).wait()
     for copy in pairs:
         copy.wait_send()
+    for condition, action in later_waits:
+        when(condition, action)
 
 
 def local(sigma_above, panels, diag_inverse, pattern, cfg_weight):
@@ -389,7 +431,7 @@
     scratch += [pltpu.VMEM((2, 2, 4 * TR, TC), F32), pltpu.VMEM((COLS, 2, 2, 4 * TR, TC), F32)]
     scratch += [pltpu.VMEM((COLS, 3, TR, TC), F32)]
     scratch += [pltpu.VMEM((W, 2, 4 * TR, TC), F32), pltpu.VMEM((W, 4 * TR, TC), F32)]
-    scratch += [pltpu.VMEM((8 * TR, 2 * FULL), BF16)] * 2
+    scratch += [pltpu.VMEM((2, 4 * TR, 2 * FULL), BF16)] * 2
     scratch += [pltpu.VMEM((3, TR, FULL), BF16)] * 2
     scratch += [pltpu.VMEM((6, GROUPS, ROWS, SUB, TC), BF16)] * 2
     scratch += [pltpu.VMEM((n * TR, FULL), BF16) for n in tiles] * 2
@@ -404,10 +446,10 @@
         pltpu.VMEM((4, 2, ROWS, TR, TC), F32),
         pltpu.VMEM((4, 4, TR, TC), F32),
         pltpu.VMEM((4, 4, TR, TC), F32),
-        pltpu.SemaphoreType.DMA((34,)),
-        pltpu.SemaphoreType.DMA((34,)),
-        pltpu.SemaphoreType.DMA((12,)),
-        pltpu.SemaphoreType.DMA((12,)),
+        pltpu.SemaphoreType.DMA((35,)),
+        pltpu.SemaphoreType.DMA((35,)),
+        pltpu.SemaphoreType.DMA((16,)),
+        pltpu.SemaphoreType.DMA((16,)),
     ]
     out = pl.pallas_call(
         kernel,

time: 117 us -> 106 us (0.906)
  Pallas kernels: 114 us -> 103 us
    pallas_call x1, Pallas kernels: 114 us -> 103 us  [local(): pl.pallas_call(kernel, name='selected_inverse', out_shape=jax.ShapeDtypeS...]
where the time goes in v3:
time: 106 us; the launch traced here: 105 us
  Pallas kernels  103 us (97%)
  local copies, waits for them, and re-layouts  1.57 us (1%)
    pallas_call x1, Pallas kernels, local(): pl.pallas_call(kernel, name='selected_inverse', out_shape=jax.ShapeDtypeS...  103 us

profile of v3, /device:TPU:6, one launch (start us, length us, event | category | flops | bytes accessed | tf_op | source)
XLA Modules:
  0.0 105.4 jit_solution(2590049756839571294)
XLA Ops:
  0.7 103.2 %selected_inverse.1 = f32[64,4,128]{2,1,0:T(4,128)} custom-call(f32[256,4,128]{2,1,0:T(4,128)} %bitcast.8, f32[4,8,64,128]{3,2,1,0:T(8,128)} %bitcast.7, f32[4,64,128]{2,1,0:T(8,128)} %bitcast.10, s32[4,8]{1,0:T(4,128)} %bitcast.11, f32[1]{0:T(128)S(6)} %copy.8.w_ref), custom_call_target="tpu_custom_call" | custom-call | tf_op jit(solution)/shard_map/selected_inverse/pallas_call | solution.py:454
  103.8 1.6 %copy.9 = f32[1,4,1,16,4,128]{5,4,3,2,1,0:T(4,128)} copy(f32[1,4,1,16,4,128]{5,4,3,2,1,0:T(4,128)} %bitcast.9) | data formatting | bytes 262144

commit v4 on v3

--- a/solution.py
+++ b/solution.py
@@ -35,11 +35,11 @@
 
 
 def kernel(
-    a_ref, u_ref, d_ref, pat_ref, w_ref, out_ref,
+    a_ref, u_ref, d_ref, pat_ref, w_hbm, out_ref,
     tr, zx0, zx1, zx2, zx3, zr, zw, az, ax, dg, qs, qr,
     ah, al, dh, dl, th, tl, zh0, zh1, zh2, zh3, zl0, zl1, zl2, zl3, bh, bl, wh, wl, qh, ql,
     pw, pa, rw, ra, gw, hb, kb,
-    send, recv, send1, recv1,
+    send, recv, send1, recv1, w_ref, w_sem,
 ):
     zx = (zx0, zx1, zx2, zx3)
     zh, zl = (zh0, zh1, zh2, zh3), (zl0, zl1, zl2, zl3)
@@ -54,6 +54,8 @@
     z_peers = [lax.rem(z_hi + d, 4) for d in range(1, 4)]
     sibling = {"cfg": 2 * z_hi + other}
 
+    weight_copy = pltpu.make_async_copy(w_hbm, w_ref, w_sem)
+    weight_copy.start()
     barrier = pltpu.get_barrier_semaphore()
     everyone = [{"row": p} for p in row_peers] + [{"col": p} for p in col_peers]
     everyone += [{"cfg": 2 * p + core} for p in z_peers] + [sibling]
@@ -205,8 +207,8 @@
 
     send_a(0)
     send_a(1)
-    send_y(3)
-
+
+    weight_copy.wait()
     weight = w_ref[0]
 
     pairs = []
@@ -270,10 +272,10 @@
         for l in range(j, W):
             start = (l - j) * TR
             part = dot3(
+                qh[start:blocks * TR, :], ql[start:blocks * TR, :],
                 zh[l][...], zl[l][...],
-                qh[start:blocks * TR, :], ql[start:blocks * TR, :],
                 (((0,), (0,)), ((), ())),
-            ).reshape(GROUPS, ROWS, SUB, TC)
+            ).T.reshape(GROUPS, ROWS, SUB, TC)
             for q in range(ROWS):
                 pw[j, l, q] = part[:, q].reshape(TR, TC)
             pw[j, l, r] += weight * d_ref[j] if l == j else inside[l - j - 1]
@@ -375,6 +377,7 @@
         if j < 2:
             send_w(j)
         if j == 2:
+            send_y(3)
             take(AZ, ax.at[c, 1 - z])
             send_a(2)
             send_a(3)
@@ -383,8 +386,9 @@
         if j == 0:
             send_x(0)
 
+    steps = {}
     column(3)
-    steps = {3: finish(3)}
+    steps[3] = finish(3)
     next(steps[3])
     take_d()
     column(2)
@@ -392,25 +396,26 @@
     next(steps[2])
     next(steps[3])
     half_column(1)
+    next(steps[2])
+    half_column(0)
     take_w(1)
-    next(steps[2])
     column(1)
     steps[1] = finish(1)
     next(steps[1])
-    next(steps[3])
     next(steps[1])
-    half_column(0)
-    next(steps[2])
     take_w(0)
     take_x(0)
     column(0)
     steps[0] = finish(0)
     next(steps[0])
+    next(steps[0])
+    next(steps[3])
+    next(steps[2])
     next(steps[1])
     next(steps[0])
-    for j in (3, 2, 1):
-        next(steps[j])
-    next(steps[0])
+    next(steps[3])
+    next(steps[2])
+    next(steps[1])
     next(steps[0])
 
     for phase, ref in waits:
@@ -450,12 +455,14 @@
         pltpu.SemaphoreType.DMA((35,)),
         pltpu.SemaphoreType.DMA((16,)),
         pltpu.SemaphoreType.DMA((16,)),
+        pltpu.SMEM((1,), F32),
+        pltpu.SemaphoreType.DMA,
     ]
     out = pl.pallas_call(
         kernel,
         name="selected_inverse",
         out_shape=jax.ShapeDtypeStruct((TR, W, TC), F32),
-        in_specs=[vmem, vmem, vmem, smem, smem],
+        in_specs=[vmem, vmem, vmem, smem, pl.BlockSpec(memory_space=pl.ANY)],
         out_specs=vmem,
         scratch_shapes=scratch,
         compiler_params=pltpu.CompilerParams(

time: 106 us -> 101 us (0.953)
  the two profiles are of different devices: /device:TPU:6 before, /device:TPU:33 now
where the time goes in v4:
time: 101 us
  Pallas kernels  98.5 us (98%)
  local copies, waits for them, and re-layouts  1.57 us (2%)
    pallas_call x1, Pallas kernels, local(): pl.pallas_call(kernel, name='selected_inverse', out_shape=jax.ShapeDtypeS...  98.5 us

profile of v4, /device:TPU:33, one launch (start us, length us, event | category | flops | bytes accessed | tf_op | source)
XLA Modules:
  0.0 100.8 jit_solution(14649666317474879883)
XLA Ops:
  0.7 98.5 %selected_inverse.1 = f32[64,4,128]{2,1,0:T(4,128)} custom-call(f32[256,4,128]{2,1,0:T(4,128)} %bitcast.8, f32[4,8,64,128]{3,2,1,0:T(8,128)} %bitcast.7, f32[4,64,128]{2,1,0:T(8,128)} %bitcast.10, s32[4,8]{1,0:T(4,128)} %bitcast.11, f32[1]{0:T(128)S(6)} %copy.8.w_hbm), custom_call_target="tpu_custom_call" | custom-call | tf_op jit(solution)/shard_map/selected_inverse/pallas_call | solution.py:461
  99.2 1.6 %copy.9 = f32[1,4,1,16,4,128]{5,4,3,2,1,0:T(4,128)} copy(f32[1,4,1,16,4,128]{5,4,3,2,1,0:T(4,128)} %bitcast.9) | data formatting | bytes 262144

commit v5 on v4

--- a/solution.py
+++ b/solution.py
@@ -35,11 +35,11 @@
 
 
 def kernel(
-    a_ref, u_ref, d_ref, pat_ref, w_hbm, out_ref,
+    a_hbm, u_hbm, d_hbm, pat_ref, w_hbm, out_ref,
     tr, zx0, zx1, zx2, zx3, zr, zw, az, ax, dg, qs, qr,
     ah, al, dh, dl, th, tl, zh0, zh1, zh2, zh3, zl0, zl1, zl2, zl3, bh, bl, wh, wl, qh, ql,
     pw, pa, rw, ra, gw, hb, kb,
-    send, recv, send1, recv1, w_ref, w_sem,
+    send, recv, send1, recv1, w_ref, w_sem, a_ref, u_ref, d_ref, in_sem,
 ):
     zx = (zx0, zx1, zx2, zx3)
     zh, zl = (zh0, zh1, zh2, zh3), (zl0, zl1, zl2, zl3)
@@ -56,6 +56,12 @@
 
     weight_copy = pltpu.make_async_copy(w_hbm, w_ref, w_sem)
     weight_copy.start()
+    u_copy = pltpu.make_async_copy(u_hbm, u_ref, in_sem.at[0])
+    a_copy = pltpu.make_async_copy(a_hbm, a_ref, in_sem.at[1])
+    d_copy = pltpu.make_async_copy(d_hbm, d_ref, in_sem.at[2])
+    u_copy.start()
+    a_copy.start()
+    d_copy.start()
     barrier = pltpu.get_barrier_semaphore()
     everyone = [{"row": p} for p in row_peers] + [{"col": p} for p in col_peers]
     everyone += [{"cfg": 2 * p + core} for p in z_peers] + [sibling]
@@ -143,13 +149,15 @@
         piece = tr.at[r, pl.ds(first, count)]
         over_rows(piece, piece, T + phase)
 
+    u_copy.wait()
     send_t(0)
     for m in range(4):
         zx[3][c, m] = -panel(W + m, 3)
     send_x(3)
     send_t(1)
-    send_t(2)
-
+
+    a_copy.wait()
+    d_copy.wait()
     source = lax.broadcasted_iota(jnp.int32, (2 * TC, 2 * TC), 0)
     target = lax.broadcasted_iota(jnp.int32, (2 * TC, 2 * TC), 1)
     parity = lax.rem(lax.div(source, SUB), 2)
@@ -367,6 +375,9 @@
             take_a(3)
             half_column(3)
             half_column(2)
+            column(3)
+            steps = {3: finish(3)}
+            next(steps[3])
         take_x(j + 1)
         minus_product(acc, j + 1, j)
         for m in range(NB - 1 - j):
@@ -377,6 +388,7 @@
         if j < 2:
             send_w(j)
         if j == 2:
+            send_t(2)
             send_y(3)
             take(AZ, ax.at[c, 1 - z])
             send_a(2)
@@ -386,10 +398,6 @@
         if j == 0:
             send_x(0)
 
-    steps = {}
-    column(3)
-    steps[3] = finish(3)
-    next(steps[3])
     take_d()
     column(2)
     steps[2] = finish(2)
@@ -429,6 +437,7 @@
 def local(sigma_above, panels, diag_inverse, pattern, cfg_weight):
     vmem = pl.BlockSpec(memory_space=pltpu.VMEM)
     smem = pl.BlockSpec(memory_space=pltpu.SMEM)
+    hbm = pl.BlockSpec(memory_space=pl.ANY)
     tiles = [NB - 1 - j for j in range(W)]
     scratch = [pltpu.VMEM((ROWS, 6, TR, TC), F32)]
     scratch += [pltpu.VMEM((COLS, n, TR, TC), F32) for n in tiles]
@@ -457,12 +466,16 @@
         pltpu.SemaphoreType.DMA((16,)),
         pltpu.SMEM((1,), F32),
         pltpu.SemaphoreType.DMA,
+        pltpu.VMEM((4 * TR, 4, TC), F32),
+        pltpu.VMEM((W, NB, TR, TC), F32),
+        pltpu.VMEM((W, TR, TC), F32),
+        pltpu.SemaphoreType.DMA((3,)),
     ]
     out = pl.pallas_call(
         kernel,
         name="selected_inverse",
         out_shape=jax.ShapeDtypeStruct((TR, W, TC), F32),
-        in_specs=[vmem, vmem, vmem, smem, pl.BlockSpec(memory_space=pl.ANY)],
+        in_specs=[hbm, hbm, hbm, smem, hbm],
         out_specs=vmem,
         scratch_shapes=scratch,
         compiler_params=pltpu.CompilerParams(

time: 101 us -> 100 us (0.990)
  the two profiles are of different devices: /device:TPU:33 before, /device:TPU:6 now
where the time goes in v5:
time: 100 us; the launch traced here: 98.3 us
  Pallas kernels  96.1 us (96%)
  local copies, waits for them, and re-layouts  1.57 us (2%)
    pallas_call x1, Pallas kernels, local(): pl.pallas_call(kernel, name='selected_inverse', out_shape=jax.ShapeDtypeS...  96.1 us

profile of v5, /device:TPU:6, one launch (start us, length us, event | category | flops | bytes accessed | tf_op | source)
XLA Modules:
  0.0 98.3 jit_solution(200855287812140480)
XLA Ops:
  0.7 96.1 %selected_inverse.1 = f32[64,4,128]{2,1,0:T(4,128)} custom-call(f32[256,4,128]{2,1,0:T(4,128)} %bitcast.8, f32[4,8,64,128]{3,2,1,0:T(8,128)} %bitcast.7, f32[4,64,128]{2,1,0:T(8,128)} %bitcast.10, s32[4,8]{1,0:T(4,128)} %bitcast.11, f32[1]{0:T(128)S(6)} %copy.8.w_hbm), custom_call_target="tpu_custom_call" | custom-call | tf_op jit(solution)/shard_map/selected_inverse/pallas_call | solution.py:474
  96.8 1.6 %copy.9 = f32[1,4,1,16,4,128]{5,4,3,2,1,0:T(4,128)} copy(f32[1,4,1,16,4,128]{5,4,3,2,1,0:T(4,128)} %bitcast.9) | data formatting | bytes 262144
